TPU v7x, 32 devices: a whole 2x2x4 slice. The times are simulated.
32 devices in a mesh: section: 16 (over z, x, core), tensor: 2 (over y).
Axes of the slice: x: 2, y: 2, z: 4, core: 2. Of those that a mesh axis runs over, the one named last changes fastest.
Arguments:
- queries: bfloat16 [2, 16, 4, 128, 3072], P(None, 'section', None, None, 'tensor'), may hold values from -6 to 6
- enc_keys: bfloat16 [2, 16, 4, 128, 3072], P(None, 'section', None, None, 'tensor'), may hold values from -6 to 6
- enc_values: bfloat16 [2, 16, 4, 128, 3072], P(None, 'section', None, None, 'tensor'), may hold values from -6 to 6
- w_query: bfloat16 [2, 16, 3072, 3072], P(None, 'section', None, 'tensor'), may hold values from -0.109375 to 0.109375
- w_out: bfloat16 [2, 16, 3072, 3072], P(None, 'section', 'tensor'), may hold values from -0.109375 to 0.109375
- arriving: bfloat16 [2, 16, 3072, 128], P(None, 'section', 'tensor'), may hold values from -6 to 6
- loss_grad: bfloat16 [2, 3, 3072, 128], P(None, None, 'tensor'), may hold values from -6 to 6
- dec_lengths: int32 [2, 16, 4, 4], P(None, 'section'), may hold values from 1 to 64, 128 in all within a row
- enc_lengths: int32 [2, 16, 4, 4], P(None, 'section'), may hold values from 1 to 64, 128 in all within a row
Outputs:
- grads: bfloat16 [2, 16, 4, 3072, 128], P(None, 'section', None, 'tensor')
Inputs may be any that keep to these rules, and one draw needn't show every extreme that they name: `dec_lengths`: each row of 4 lengths sums to 128, and its largest is 64. `enc_lengths`: each row of 4 lengths sums to 128, and its largest is 64.
All inputs are finite; a program needn't handle non-finite values.
Results may differ from a plain program's by a relative error of at most 0.012.
Values may be sent and summed in bfloat16 or wider, within the bound.
A program may use at most 192 MiB of HBM per device.

v0:
```python
import functools

import jax
import jax.numpy as jnp
from jax import lax
from jax.experimental import pallas as pl
from jax.experimental.pallas import tpu as pltpu
from jax.sharding import PartitionSpec as P

HEAD = 128
CHUNK = 384
MESH = pl.DeviceIdType.MESH


def largest_divisor(total, limit):
    return max(size for size in range(1, min(total, limit) + 1) if total % size == 0)


def relay_kernel(
    sections, group, dims,
    dec_ref, enc_ref, q_hbm, k_hbm, v_hbm, wq_hbm, wo_hbm, arriving_ref, loss_ref,
    out_ref,
    wq, wo, qs, ks, vs, entering, attn, dqt, part, landed,
    wq_sem, wo_sem, qkv_sem, enter_sem, feed_send, next_send, rs_send, rs_recv,
):
    ticks, seq, inner, width, rows, chunk = dims
    chunks = rows // chunk
    section = lax.axis_index("section")
    me = lax.axis_index("tensor")

    def peer(step):
        return lax.rem(me + step, group)

    def load_qkv(c, t):
        return [
            pltpu.make_async_copy(hbm.at[c, t], vmem.at[c], qkv_sem.at[c, which])
            for which, (hbm, vmem) in enumerate(((q_hbm, qs), (k_hbm, ks), (v_hbm, vs)))
        ]

    def load_wo(c):
        return pltpu.make_async_copy(wo_hbm.at[c], wo.at[c], wo_sem.at[c])

    def load_wq(c):
        return pltpu.make_async_copy(wq_hbm.at[c], wq.at[c], wq_sem.at[c])

    for c in range(2):
        load_wo(c).start()
        for copy in load_qkv(c, 0):
            copy.start()
        load_wq(c).start()

    barrier = pltpu.get_barrier_semaphore()
    for step in range(1, group):
        pl.semaphore_signal(
            barrier, inc=1, device_id=(section, peer(step)), device_id_type=MESH
        )

    @pl.when(section > 0)
    def _():
        for step in range(group):
            pl.semaphore_signal(
                barrier, inc=1, device_id=(section - 1, peer(step)), device_id_type=MESH
            )

    @pl.when(section < sections - 1)
    def _():
        for step in range(group):
            pl.semaphore_signal(
                barrier, inc=1, device_id=(section + 1, peer(step)), device_id_type=MESH
            )

    around = (section > 0).astype(jnp.int32) + (section < sections - 1).astype(jnp.int32)
    pl.semaphore_wait(barrier, group - 1 + group * around)

    def place(source, k):
        return pl.ds(pl.multiple_of(source * rows + k * chunk, chunk), chunk)

    def here(k):
        return pl.ds(pl.multiple_of(k * chunk, chunk), chunk)

    def feed_copy(source, c, t, k, step):
        return pltpu.make_async_remote_copy(
            src_ref=source,
            dst_ref=entering.at[t, c, place(me, k)],
            send_sem=feed_send.at[t, c, k, step],
            recv_sem=enter_sem.at[t, c, k, me],
            device_id=(section, peer(step)),
            device_id_type=MESH,
        )

    def feed(source, c, t, k):
        for step in range(1, group):
            feed_copy(source, c, t, k, step).start()
        pltpu.make_async_copy(
            source, entering.at[t, c, place(me, k)], enter_sem.at[t, c, k, me]
        ).start()

    def next_copy(c, t, k, step):
        return pltpu.make_async_remote_copy(
            src_ref=out_ref.at[c, t, here(k)],
            dst_ref=entering.at[t + 1, c, place(me, k)],
            send_sem=next_send.at[t, c, k, step],
            recv_sem=enter_sem.at[t + 1, c, k, me],
            device_id=(section + 2 * c - 1, peer(step)),
            device_id_type=MESH,
        )

    def reduce_copy(c, t, k, step):
        return pltpu.make_async_remote_copy(
            src_ref=part.at[c, place(peer(step), k)],
            dst_ref=landed.at[t, c, step - 1, here(k)],
            send_sem=rs_send.at[t, c, k, step - 1],
            recv_sem=rs_recv.at[t, c, k, step - 1],
            device_id=(section, peer(step)),
            device_id_type=MESH,
        )

    def goes_on(c, t):
        target = section + 2 * c - 1
        return (target >= 0) & (target < sections) & (t + 1 < ticks)

    def begins(c, t):
        origin = section - 2 * c + 1
        return ((origin < 0) | (origin >= sections)) & (t + 1 < ticks)

    for c in range(2):
        for k in range(chunks):
            feed(arriving_ref.at[c, here(k)], c, 0, k)

    def finish(c, t, k):
        total = (
            entering[t, c, place(me, k), :].astype(jnp.float32)
            + part[c, place(me, k), :].astype(jnp.float32)
        )
        for step in range(1, group):
            copy = reduce_copy(c, t, k, step)
            copy.wait_send()
            copy.wait_recv()
            total += landed[t, c, step - 1, here(k), :].astype(jnp.float32)
        out_ref[c, t, here(k), :] = total.astype(jnp.bfloat16)

        @pl.when(goes_on(c, t))
        def _():
            for step in list(range(1, group)) + [0]:
                next_copy(c, t, k, step).start()

        @pl.when(begins(c, t))
        def _():
            feed(loss_ref.at[c, jnp.minimum(t, ticks - 2), here(k)], c, t + 1, k)

    tile = largest_divisor(inner, 384)
    heads = inner // HEAD
    unroll = largest_divisor(heads, 4)

    def doc_ids(lens, base, axis):
        places = lax.broadcasted_iota(jnp.int32, (seq, seq), axis)
        first = lens[base]
        second = first + lens[base + 1]
        third = second + lens[base + 2]
        return (
            (places >= first).astype(jnp.int32)
            + (places >= second).astype(jnp.int32)
            + (places >= third).astype(jnp.int32)
        )

    def phase(index, carry):
        c = lax.rem(index, 2)
        t = index // 2
        for k in range(chunks):
            for source in range(group):
                pltpu.make_async_copy(
                    entering.at[t, c, place(source, k)],
                    entering.at[t, c, place(source, k)],
                    enter_sem.at[t, c, k, source],
                ).wait()

        @pl.when(t == 0)
        def _():
            load_wo(c).wait()

        def out_tile(r, carry):
            span = pl.ds(pl.multiple_of(r * tile, tile), tile)
            attn[span, :] = jnp.dot(
                wo[c, span, :], entering[t, c], preferred_element_type=jnp.float32
            ).astype(jnp.bfloat16)
            return carry

        lax.fori_loop(0, inner // tile, out_tile, 0)
        for copy in load_qkv(c, t):
            copy.wait()
        base = (c * ticks + t) * 4
        allowed = doc_ids(enc_ref, base, 0) == doc_ids(dec_ref, base, 1)

        def head_group(g, carry):
            for within in range(unroll):
                span = pl.ds(pl.multiple_of((g * unroll + within) * HEAD, HEAD), HEAD)
                key = ks[c, :, span]
                scores = lax.dot_general(
                    key, qs[c, :, span], (((1,), (1,)), ((), ())),
                    preferred_element_type=jnp.float32,
                ) * HEAD ** (-0.5)
                scores = jnp.where(allowed, scores, -1e30)
                top = jnp.max(scores, axis=0, keepdims=True)
                weights = jnp.exp(scores - top)
                weights = weights * (1.0 / jnp.sum(weights, axis=0, keepdims=True))
                prob_grad = jnp.dot(
                    vs[c, :, span], attn[span, :], preferred_element_type=jnp.float32
                )
                rowdot = jnp.sum(weights * prob_grad, axis=0, keepdims=True)
                score_grad = (weights * (prob_grad - rowdot)).astype(jnp.bfloat16)
                dqt[span, :] = (
                    lax.dot_general(
                        key, score_grad, (((0,), (0,)), ((), ())),
                        preferred_element_type=jnp.float32,
                    ) * HEAD ** (-0.5)
                ).astype(jnp.bfloat16)
            return carry

        lax.fori_loop(0, heads // unroll, head_group, 0)

        @pl.when(t + 1 < ticks)
        def _():
            for copy in load_qkv(c, jnp.minimum(t + 1, ticks - 1)):
                copy.start()

        @pl.when(t == 0)
        def _():
            load_wq(c).wait()

        def head_term(source, k):
            span = place(source, k)
            part[c, span, :] = jnp.dot(
                wq[c, span, :], dqt[...], preferred_element_type=jnp.float32
            ).astype(jnp.bfloat16)

        def send_chunk(k, carry):
            @pl.when(index > 0)
            def _():
                before = jnp.maximum(index - 1, 0)
                finish(lax.rem(before, 2), before // 2, k)

            for step in range(1, group):
                head_term(peer(step), k)
                reduce_copy(c, t, k, step).start()
            return carry

        lax.fori_loop(0, chunks, send_chunk, 0)

        def own_chunk(k, carry):
            head_term(me, k)
            return carry

        lax.fori_loop(0, chunks, own_chunk, 0)
        return carry

    lax.fori_loop(0, 2 * ticks, phase, 0)

    def last_chunk(k, carry):
        finish(1, ticks - 1, k)
        return carry

    lax.fori_loop(0, chunks, last_chunk, 0)

    def drain(index, carry):
        c = lax.rem(index, 2)
        t = index // 2

        @pl.when(t == 0)
        def _():
            for k in range(chunks):
                for step in range(1, group):
                    feed_copy(arriving_ref.at[c, here(k)], c, 0, k, step).wait_send()

        @pl.when(goes_on(c, t))
        def _():
            for k in range(chunks):
                for step in range(group):
                    next_copy(c, t, k, step).wait_send()

        @pl.when(begins(c, t))
        def _():
            for k in range(chunks):
                for step in range(1, group):
                    feed_copy(
                        loss_ref.at[c, jnp.minimum(t, ticks - 2), here(k)], c, t + 1, k, step
                    ).wait_send()

        return carry

    lax.fori_loop(0, 2 * ticks, drain, 0)


def local(
    queries, enc_keys, enc_values, w_query, w_out, arriving, loss_grad, dec_lengths, enc_lengths
):
    sections = lax.axis_size("section")
    group = lax.axis_size("tensor")
    _, _, ticks, seq, inner = queries.shape
    width = w_query.shape[2]
    rows = arriving.shape[2]
    chunk = largest_divisor(rows, CHUNK)
    chunks = rows // chunk
    bf16 = jnp.bfloat16
    vmem = pl.BlockSpec(memory_space=pltpu.VMEM)
    smem = pl.BlockSpec(memory_space=pltpu.SMEM)
    anywhere = pl.BlockSpec(memory_space=pl.ANY)
    dma = pltpu.SemaphoreType.DMA
    grads = pl.pallas_call(
        functools.partial(
            relay_kernel, sections, group, (ticks, seq, inner, width, rows, chunk)
        ),
        out_shape=jax.ShapeDtypeStruct((2, ticks, rows, seq), bf16),
        in_specs=[smem, smem] + [anywhere] * 7,
        out_specs=vmem,
        scratch_shapes=[
            pltpu.VMEM((2, width, inner), bf16),
            pltpu.VMEM((2, inner, width), bf16),
            pltpu.VMEM((2, seq, inner), bf16),
            pltpu.VMEM((2, seq, inner), bf16),
            pltpu.VMEM((2, seq, inner), bf16),
            pltpu.VMEM((ticks, 2, width, seq), bf16),
            pltpu.VMEM((inner, seq), bf16),
            pltpu.VMEM((inner, seq), bf16),
            pltpu.VMEM((2, width, seq), bf16),
            pltpu.VMEM((ticks, 2, group - 1, rows, seq), bf16),
            dma((2,)),
            dma((2,)),
            dma((2, 3)),
            dma((ticks, 2, chunks, group)),
            dma((ticks, 2, chunks, group)),
            dma((ticks, 2, chunks, group)),
            dma((ticks, 2, chunks, group - 1)),
            dma((ticks, 2, chunks, group - 1)),
        ],
        compiler_params=pltpu.CompilerParams(
            collective_id=0, has_side_effects=True, vmem_limit_bytes=60 * 1024 * 1024
        ),
        cost_estimate=pl.CostEstimate(
            flops=4 * ticks * inner * (2 * width + 3 * seq) * seq,
            bytes_accessed=2 * (4 * width * inner + 6 * ticks * seq * inner),
            transcendentals=2 * ticks * seq * inner,
        ),
    )(
        dec_lengths.reshape(-1),
        enc_lengths.reshape(-1),
        queries[:, 0],
        enc_keys[:, 0],
        enc_values[:, 0],
        w_query[:, 0],
        w_out[:, 0],
        arriving[:, 0],
        loss_grad,
    )
    return grads[:, None]


def solution(mesh):
    in_specs = (
        P(None, "section", None, None, "tensor"),
        P(None, "section", None, None, "tensor"),
        P(None, "section", None, None, "tensor"),
        P(None, "section", None, "tensor"),
        P(None, "section", "tensor", None),
        P(None, "section", "tensor", None),
        P(None, None, "tensor", None),
        P(None, "section", None, None),
        P(None, "section", None, None),
    )
    out_specs = P(None, "section", None, "tensor", None)
    return jax.shard_map(local, mesh=mesh, in_specs=in_specs, out_specs=out_specs, check_vma=False)
```

profile of v0, /device:TPU:0, one launch (start us, length us, event | category | flops | bytes accessed | tf_op | source)
XLA Modules:
  0.0 174.4 jit_solution(13271580405143508582)
XLA Ops:
  0.0 1.3 reshape.6.dec_ref
  1.3 1.2 reshape.7.enc_ref
  2.5 168.1 %shard_map.91 = bf16[2,4,1536,128]{3,2,1,0:T(8,128)(2,1)} custom-call(s32[32]{0:T(128)} %reshape.6.dec_ref, s32[32]{0:T(128)} %reshape.7.enc_ref, bf16[2,4,128,1536]{3,2,1,0:T(8,128)(2,1)} %bitcast.12, bf16[2,4,128,1536]{3,2,1,0:T(8,128)(2,1)} %bitcast.13, bf16[2,4,128,1536]{3,2,1,0:T(8,128)(2,1)} %bitcast.14, bf16[2,3072,1536]{2,1,0:T(8,128)(2,1)} %bitcast.10, ...), custom_call_target="tpu_custom_call" | custom-call | flops 20535312384 | bytes 47185920 | tf_op jit(solution)/shard_map/pallas_call | solution.py:308
  170.6 3.8 %copy.12 = bf16[2,1,4,1536,128]{4,3,2,1,0:T(8,128)(2,1)} copy(bf16[2,1,4,1536,128]{4,3,2,1,0:T(8,128)(2,1)} %bitcast.9) | data formatting | bytes 6291456
where the time goes:
time: 175 us; the launch traced here: 174 us
  Pallas kernels  168 us (96%)
  local copies, waits for them, and re-layouts  6.31 us (4%)
    pallas_call x1, Pallas kernels, local(): pl.pallas_call(functools.partial(relay_kernel, sections, group, (ticks, s...  168 us
    unnamed x1, local copies, waits for them, and re-layouts  3.78 us

commit v1 on v0

--- a/solution.py
+++ b/solution.py
@@ -8,7 +8,7 @@
 from jax.sharding import PartitionSpec as P
 
 HEAD = 128
-CHUNK = 384
+CHUNK = 768
 MESH = pl.DeviceIdType.MESH
 
 
@@ -148,15 +148,16 @@
         def _():
             feed(loss_ref.at[c, jnp.minimum(t, ticks - 2), here(k)], c, t + 1, k)
 
-    tile = largest_divisor(inner, 384)
+    tile = largest_divisor(inner, 768)
     heads = inner // HEAD
-    unroll = largest_divisor(heads, 4)
+    unroll = largest_divisor(heads, 12)
 
     def doc_ids(lens, base, axis):
         places = lax.broadcasted_iota(jnp.int32, (seq, seq), axis)
-        first = lens[base]
-        second = first + lens[base + 1]
-        third = second + lens[base + 2]
+        c, t = base
+        first = lens[c, 0, t, 0]
+        second = first + lens[c, 0, t, 1]
+        third = second + lens[c, 0, t, 2]
         return (
             (places >= first).astype(jnp.int32)
             + (places >= second).astype(jnp.int32)
@@ -178,6 +179,13 @@
         def _():
             load_wo(c).wait()
 
+        def finish_before(low, high):
+            @pl.when(index > 0)
+            def _():
+                before = jnp.maximum(index - 1, 0)
+                for k in range(low, high):
+                    finish(lax.rem(before, 2), before // 2, k)
+
         def out_tile(r, carry):
             span = pl.ds(pl.multiple_of(r * tile, tile), tile)
             attn[span, :] = jnp.dot(
@@ -188,7 +196,7 @@
         lax.fori_loop(0, inner // tile, out_tile, 0)
         for copy in load_qkv(c, t):
             copy.wait()
-        base = (c * ticks + t) * 4
+        base = (c, t)
         allowed = doc_ids(enc_ref, base, 0) == doc_ids(dec_ref, base, 1)
 
         def head_group(g, carry):
@@ -216,7 +224,9 @@
                 ).astype(jnp.bfloat16)
             return carry
 
+        finish_before(0, chunks // 2)
         lax.fori_loop(0, heads // unroll, head_group, 0)
+        finish_before(chunks // 2, chunks)
 
         @pl.when(t + 1 < ticks)
         def _():
@@ -234,11 +244,6 @@
             ).astype(jnp.bfloat16)
 
         def send_chunk(k, carry):
-            @pl.when(index > 0)
-            def _():
-                before = jnp.maximum(index - 1, 0)
-                finish(lax.rem(before, 2), before // 2, k)
-
             for step in range(1, group):
                 head_term(peer(step), k)
                 reduce_copy(c, t, k, step).start()
@@ -341,8 +346,8 @@
             transcendentals=2 * ticks * seq * inner,
         ),
     )(
-        dec_lengths.reshape(-1),
-        enc_lengths.reshape(-1),
+        dec_lengths,
+        enc_lengths,
         queries[:, 0],
         enc_keys[:, 0],
         enc_values[:, 0],

time: 175 us -> 150 us (0.86)
  Pallas kernels: 168 us -> 145 us
  local copies, waits for them, and re-layouts: 6.31 us -> 3.78 us
    pallas_call x1, Pallas kernels: 168 us -> 145 us  [local(): pl.pallas_call(functools.partial(relay_kernel, sections, group, (ticks, s...]
    reshape x2 -> x0, local copies, waits for them, and re-layouts: 2.53 us -> none  [the longest x1 1.28 us: local(): dec_lengths.reshape(-1)]
where the time goes in v1:
time: 150 us; the launch traced here: 149 us
  Pallas kernels  145 us (97%)
  local copies, waits for them, and re-layouts  3.78 us (3%)
    pallas_call x1, Pallas kernels, local(): pl.pallas_call(functools.partial(relay_kernel, sections, group, (ticks, s...  145 us
    unnamed x1, local copies, waits for them, and re-layouts  3.78 us

profile of v1, /device:TPU:0, one launch (start us, length us, event | category | flops | bytes accessed | tf_op | source)
XLA Modules:
  0.0 149.0 jit_solution(4524130128399658544)
XLA Ops:
  0.0 145.2 %shard_map.91 = bf16[2,4,1536,128]{3,2,1,0:T(8,128)(2,1)} custom-call(s32[2,1,4,4]{3,2,1,0:T(4,128)} %dec_ref.1, s32[2,1,4,4]{3,2,1,0:T(4,128)} %enc_ref.1, bf16[2,4,128,1536]{3,2,1,0:T(8,128)(2,1)} %bitcast.12, bf16[2,4,128,1536]{3,2,1,0:T(8,128)(2,1)} %bitcast.13, bf16[2,4,128,1536]{3,2,1,0:T(8,128)(2,1)} %bitcast.14, bf16[2,3072,1536]{2,1,0:T(8,128)(2,1)} %bitcast.10, ...), custom_call_target="tpu_custom_call" | custom-call | flops 20535312384 | bytes 47185920 | tf_op jit(solution)/shard_map/pallas_call | solution.py:313
  145.2 3.8 %copy.12 = bf16[2,1,4,1536,128]{4,3,2,1,0:T(8,128)(2,1)} copy(bf16[2,1,4,1536,128]{4,3,2,1,0:T(8,128)(2,1)} %bitcast.9) | data formatting | bytes 6291456
